TPU v7x, 256 devices: a whole 4x4x8 slice. The times are simulated.
256 devices in a mesh: rows: 4 (over y_hi, core), cols: 64 (over y_lo, x, z).
Axes of the slice: x: 4, y: 4 (y_hi: 2, y_lo: 2; y = y_hi * 2 + y_lo), z: 8, core: 2. Of those that a mesh axis runs over, the one named last changes fastest.
Arguments:
- features: bfloat16 [128, 8192, 384], P('rows', 'cols'), may hold values from -6 to 6
- depth_weight: float32 [7, 7, 384], replicated, may hold values from -0.875 to 0.875
- depth_bias: float32 [384], replicated, may hold values from -3 to 3
- norm_gain: float32 [384], replicated, may hold values from 0.1 to 1.9
- norm_shift: float32 [384], replicated, may hold values from -2 to 2
- expand_weight: bfloat16 [384, 1536], replicated, may hold values from -0.3125 to 0.3125
- expand_bias: float32 [1536], replicated, may hold values from -3 to 3
- reduce_weight: bfloat16 [1536, 384], replicated, may hold values from -0.15625 to 0.15625
- reduce_bias: float32 [384], replicated, may hold values from -3 to 3
- layer_scale: float32 [384], replicated, may hold values from 0.3 to 1.5
- down_gain: float32 [384], replicated, may hold values from 0.1 to 1.9
- down_shift: float32 [384], replicated, may hold values from -2 to 2
- down_weight: bfloat16 [2, 2, 384, 768], replicated, may hold values from -0.15625 to 0.15625
- down_bias: float32 [768], replicated, may hold values from -3 to 3
Outputs:
- next_section: bfloat16 [64, 4096, 768], P(None, 'cols', 'rows')
All inputs are finite; a program needn't handle non-finite values.
Results may differ from a plain program's by a relative error of at most 0.0059.
Values may be sent and summed in bfloat16 or wider, within the bound.
A program may use at most 128 MiB of HBM per device.

v0:
```python
import jax
import jax.numpy as jnp
from jax import lax
from jax.sharding import PartitionSpec as P


def with_halo(cells, sides, width):
    for axis, dim in sides:
        count = lax.axis_size(axis)
        ends = count - 1
        head = lax.slice_in_dim(cells, 0, width, axis=dim)
        tail = lax.slice_in_dim(cells, cells.shape[dim] - width, cells.shape[dim], axis=dim)
        cells = jnp.concatenate(
            [
                lax.ppermute(tail, axis, [(i, (i + 1) % count) for i in range(ends)]),
                cells,
                lax.ppermute(head, axis, [((i + 1) % count, i) for i in range(ends)]),
            ],
            axis=dim,
        )
    return cells


def layer_norm(values, gain, shift):
    center = jnp.mean(values, axis=-1, keepdims=True)
    spread = jnp.mean((values - center) ** 2, axis=-1, keepdims=True)
    return (values - center) * lax.rsqrt(spread + 1e-06) * gain + shift


def per_device(
    features,
    depth_weight,
    depth_bias,
    norm_gain,
    norm_shift,
    expand_weight,
    expand_bias,
    reduce_weight,
    reduce_bias,
    layer_scale,
    down_gain,
    down_shift,
    down_weight,
    down_bias,
):
    tile_rows, tile_cols, channels = features.shape
    padded = with_halo(features, (("rows", 0), ("cols", 1)), 3)
    total = jnp.broadcast_to(depth_bias, (tile_rows, tile_cols, channels))
    for offset_a in range(7):
        for offset_b in range(7):
            window = padded[
                offset_a : offset_a + tile_rows, offset_b : offset_b + tile_cols
            ].astype(jnp.float32)
            total = total + window * depth_weight[offset_a, offset_b]
    normed = (
        layer_norm(total, norm_gain, norm_shift)
        .astype(jnp.bfloat16)
        .reshape(tile_rows * tile_cols, channels)
    )
    hidden = jax.nn.gelu(
        jnp.dot(normed, expand_weight, preferred_element_type=jnp.float32) + expand_bias,
        approximate=False,
    ).astype(jnp.bfloat16)
    branch = jnp.dot(hidden, reduce_weight, preferred_element_type=jnp.float32) + reduce_bias
    source = features.reshape(tile_rows * tile_cols, channels).astype(jnp.float32)
    block_out = (source + layer_scale * branch).astype(jnp.bfloat16)
    down_normed = layer_norm(block_out.astype(jnp.float32), down_gain, down_shift).astype(
        jnp.bfloat16
    )
    half_rows = tile_rows // 2
    half_cols = tile_cols // 2
    patches = (
        down_normed.reshape(half_rows, 2, half_cols, 2, channels)
        .transpose(0, 2, 1, 3, 4)
        .reshape(half_rows, half_cols, 4 * channels)
    )
    out_channels = down_weight.shape[3]
    flat_weight = down_weight.reshape(4 * channels, out_channels)
    result = (
        jnp.dot(
            patches.reshape(half_rows * half_cols, 4 * channels),
            flat_weight,
            preferred_element_type=jnp.float32,
        )
        + down_bias
    )
    result = result.astype(jnp.bfloat16).reshape(half_rows, half_cols, out_channels)
    return lax.all_to_all(result, "rows", split_axis=2, concat_axis=0, tiled=True)


def solution(mesh):
    in_specs = (
        P("rows", "cols", None),
        P(),
        P(),
        P(),
        P(),
        P(),
        P(),
        P(),
        P(),
        P(),
        P(),
        P(),
        P(),
        P(),
    )
    out_specs = P(None, "cols", "rows")
    return jax.shard_map(
        per_device, mesh=mesh, in_specs=in_specs, out_specs=out_specs, check_vma=False
    )
```

profile of v0, /device:TPU:8, one launch (start us, length us, event | category | flops | bytes accessed | tf_op | source)
XLA Modules:
  0.0 287.7 jit_solution(10233040631761055658)
XLA Ops:
  0.0 0.0 copy-start
  0.0 1.3 fusion.121
  1.3 1.8 collective-permute-start
  3.0 1.3 collective-permute-start.1
  4.3 1.3 slice_reduce_fusion.48
  5.7 1.2 slice_reduce_fusion.47
  6.9 0.0 collective-permute-done
  6.9 0.8 constant_dynamic-update-slice_fusion.4
  7.7 0.0 copy-start.4
  7.7 6.1 %constant_dynamic-update-slice_fusion.3 = (bf16[35,128,384]{2,1,0:T(8,128)(2,1)}, bf16[38,128,384]{2,1,0:T(8,128)(2,1)S(1)}, bf16[35,128,384]{2,1,0:T(8,128)(2,1)}) fusion(bf16[35,128,384]{2,1,0:T(8,128)(2,1)} %get-tuple-element.63, bf16[32,128,384]{2,1,0:T(8,128)(2,1)} %param.14, bf16[38,128,384]{2,1,0:T(8,128)(2,1)S(1)} %get-tuple-element.64), kind=kLoop, calls=%fused_computation.166 | loop fusion | bytes 12582912 | tf_op jit(solution)/shard_map/concatenate | solution.py:13
  13.8 0.0 collective-permute-done.1
  13.8 0.8 constant_dynamic-update-slice_fusion.5
  14.6 0.0 copy-start.3
  14.6 1.9 copy-done.3
  16.5 0.1 fusion.120
  16.6 9.8 %collective-permute-start.3 = (bf16[38,3,384]{2,1,0:T(4,128)(2,1)S(1)}, bf16[38,3,384]{2,1,0:T(4,128)(2,1)S(1)}, u32[]{:S(2)}, u32[]{:S(2)}) collective-permute-start(bf16[38,3,384]{2,1,0:T(4,128)(2,1)S(1)} %get-tuple-element.57), channel_id=1, source_target_pairs={{1,0},{2,1},{3,2},{4,3},{5,4},{6,5},{7,6},{8,7},{9,8},{10,9},{11,1... | collective-permute-start | bytes 262664 | tf_op jit(solution)/shard_map/ppermute | solution.py:17
  26.4 1.9 collective-permute-start.2
  28.4 1.0 slice_reduce_fusion.46
  29.3 0.0 collective-permute-done.3
  29.3 8.0 %collective-permute-done.2 = bf16[38,3,384]{2,1,0:T(4,128)(2,1)S(1)} collective-permute-done((bf16[38,3,384]{2,1,0:T(4,128)(2,1)S(1)}, bf16[38,3,384]{2,1,0:T(4,128)(2,1)S(1)}, u32[]{:S(2)}, u32[]{:S(2)}) %collective-permute-start.2) | collective-permute-done | bytes 87584 | tf_op jit(solution)/shard_map/ppermute | solution.py:15
  37.4 0.0 copy-done.4
  37.4 94.6 %fusion.119 = (f32[32,128]{1,0:T(8,128)S(1)}, f32[32,128,384]{2,1,0:T(8,128)}) fusion(f32[384]{0:T(512)S(1)} %get-tuple-element.52, bf16[38,3,384]{2,1,0:T(4,128)(2,1)S(1)} %collective-permute-done.3, bf16[38,128,384]{2,1,0:T(8,128)(2,1)} %copy-done.3, f32[384]{0:T(512)S(1)} %get-tuple-element.53, f32[384]{0:T(512)S(1)} %get-tuple-element.6, ...), kind=kLoop, calls=%fused_computation.253 | loop fusion | flops 430960640 | bytes 32315392 | tf_op jit(solution)/shard_map/reduce_sum | solution.py:25
  132.0 0.0 copy-start.1
  132.0 0.0 copy-start.5
  132.0 0.0 copy-start.6
  132.0 3.7 %multiply_reduce_fusion = f32[32,128]{1,0:T(8,128)S(1)} fusion(f32[32,128,384]{2,1,0:T(8,128)} %get-tuple-element.55, f32[32,128]{1,0:T(8,128)S(1)} %broadcast_multiply_fusion.1), kind=kLoop, calls=%fused_computation.102 | loop fusion | flops 4714496 | bytes 6324224 | tf_op jit(solution)/shard_map/reduce_sum | solution.py:26
  135.8 0.0 copy-start.9
  135.8 0.0 copy-start.11
  135.8 0.8 copy-done.1
  136.6 0.0 copy-done.5
  136.6 0.0 copy-done.6
  136.6 1.5 add_convert_fusion
  138.1 0.0 copy-done.9
  138.1 0.0 copy-done.11
  138.1 0.0 copy-start.2
  138.1 0.0 copy-start.10
  138.2 0.0 copy-start.13
  138.2 0.0 copy-start.14
  138.2 59.8 %fusion.2.clone.3.clone.4 = bf16[4096,1536]{1,0:T(8,128)(2,1)S(1)} fusion(bf16[4096,384]{1,0:T(8,128)(2,1)S(1)} %bitcast.33, bf16[384,1536]{1,0:T(8,128)(2,1)S(1)} %copy-done.9, f32[1536]{0:T(1024)S(1)} %copy-done.11), kind=kOutput, calls=%fused_computation.43.clone.clone.clone.clone.clone.clone.clone.1 | convolution fusion | flops 5247074304 | bytes 16914432 | tf_op jit(solution)/shard_map/dot_general | solution.py:61
  197.9 0.0 copy-done.2
  198.0 0.0 copy-done.10
  198.0 0.0 copy-done.13
  198.0 0.0 copy-done.14
  198.0 0.0 copy-start.7
  198.0 0.0 copy-start.8
  198.0 7.6 %convert_reduce_fusion = (f32[4096]{0:T(1024)S(1)}, bf16[4096,384]{1,0:T(8,128)(2,1)S(1)}) fusion(f32[384]{0:T(512)S(1)} %copy-done.13, bf16[1536,384]{1,0:T(8,128)(2,1)S(1)} %copy-done.10, f32[384]{0:T(512)S(1)} %copy-done.14, bf16[32,128,384]{2,1,0:T(8,128)(2,1)S(1)} %copy-done.2, bf16[4096,1536]{1,0:T(8,128)(2,1)S(1)} %fusion.2.clone.3.clone.4), kind=kOutput, calls=%fused_computation.92 | convolution fusion | flops 4842844160 | bytes 20073472 | tf_op jit(solution)/shard_map/dot_general | solution.py:64
  205.6 1.7 fusion.44
  207.3 0.0 copy-done.7
  207.3 0.0 copy-done.8
  207.3 3.7 %fusion.47 = bf16[4096,384]{1,0:T(8,128)(2,1)} fusion(bf16[4096,384]{1,0:T(8,128)(2,1)S(1)} %get-tuple-element.68, f32[384]{0:T(512)S(1)} %copy-done.7, f32[384]{0:T(512)S(1)} %copy-done.8, f32[4096]{0:T(1024)S(1)} %add_rsqrt_fusion, f32[4096]{0:T(1024)S(1)} %broadcast_multiply_fusion), kind=kLoop, calls=%fused_computation.98 | loop fusion | flops 9437184 | bytes 6327296 | tf_op jit(solution)/shard_map/convert_element_type | solution.py:67
  211.0 7.3 %reshape.48 = bf16[16,2,64,2,384]{4,3,2,1,0:T(2,128)(2,1)} reshape(bf16[4096,384]{1,0:T(8,128)(2,1)} %fusion.47) | data formatting | bytes 6291456 | tf_op jit(solution)/shard_map/reshape | solution.py:73
  218.3 0.0 copy-start.12
  218.3 5.9 %copy.22 = bf16[16,2,64,2,384]{4,3,1,2,0:T(2,128)(2,1)} copy(bf16[16,2,64,2,384]{4,3,2,1,0:T(2,128)(2,1)} %reshape.48) | data formatting | bytes 6291456 | tf_op jit(solution)/shard_map/reshape | solution.py:73
  224.2 8.0 %reshape_reshape.3 = bf16[1024,1536]{1,0:T(8,128)(2,1)} reshape(bf16[16,64,2,2,384]{4,3,2,1,0:T(2,128)(2,1)} %bitcast.30) | data formatting | bytes 6291456 | tf_op jit(solution)/shard_map/reshape;reshape | solution.py:81
  232.2 0.0 copy-done
  232.2 0.0 copy-done.12
  232.2 5.6 %add_convert_fusion.1 = bf16[1024,768]{1,0:T(8,128)(2,1)} fusion(bf16[1024,1536]{1,0:T(8,128)(2,1)} %reshape_reshape.3, bf16[1536,768]{1,0:T(8,128)(2,1)S(1)} %bitcast.29, f32[768]{0:T(1024)S(1)} %copy-done.12), kind=kOutput, calls=%fused_computation.162 | convolution fusion | flops 2417491968 | bytes 7080960 | tf_op jit(solution)/shard_map/dot_general | solution.py:80
  237.9 5.2 %copy.19 = bf16[16,64,768]{1,0,2:T(8,128)(2,1)} copy(bf16[16,64,768]{2,1,0:T(8,128)(2,1)} %bitcast.34) | data formatting | bytes 3145728 | tf_op jit(solution)/shard_map/reshape | solution.py:87
  243.1 5.0 %reshape.101 = bf16[4,2,98304]{2,1,0:T(2,128)(2,1)} reshape(bf16[768,16,64]{2,1,0:T(8,128)(2,1)} %bitcast.31) | data formatting | bytes 3145728
  248.1 29.6 %all_to_all.18 = bf16[4,2,98304]{2,1,0:T(2,128)(2,1)} all-to-all(bf16[4,2,98304]{2,1,0:T(2,128)(2,1)} %reshape.101), channel_id=1, replica_groups=mesh['rows'=4,'cols'=64] {'rows'}, dimensions={0} | all-to-all | bytes 3145728 | tf_op jit(solution)/shard_map/all_to_all | solution.py:88
  277.7 4.9 %reshape.102 = bf16[768,16,64]{2,1,0:T(8,128)(2,1)} reshape(bf16[4,2,98304]{2,1,0:T(2,128)(2,1)} %all_to_all.18) | data formatting | bytes 3145728
  282.6 5.1 %copy.20 = bf16[4,16,64,192]{3,2,1,0:T(8,128)(2,1)} copy(bf16[4,16,64,192]{2,1,3,0:T(8,128)(2,1)} %bitcast.32) | data formatting | bytes 3145728 | tf_op jit(solution)/shard_map/all_to_all | solution.py:88
  (4 shorter events, 0.0 us)
Async XLA Ops:
  0.0 232.2 %copy-start = (bf16[2,2,384,768]{3,2,1,0:T(8,128)(2,1)S(1)}, bf16[2,2,384,768]{3,2,1,0:T(8,128)(2,1)}, u32[]{:S(2)}) copy-start(bf16[2,2,384,768]{3,2,1,0:T(8,128)(2,1)} %param.26) | copy-start | bytes 7077892
  1.3 5.6 %collective-permute-start = (bf16[3,128,384]{2,1,0:T(8,128)(2,1)S(1)}, bf16[3,128,384]{2,1,0:T(8,128)(2,1)S(1)}, u32[]{:S(2)}, u32[]{:S(2)}) collective-permute-start(bf16[3,128,384]{2,1,0:T(8,128)(2,1)S(1)} %get-tuple-element.62), channel_id=1, source_target_pairs={{0,64},{64,128},{128,192},{1,65},{65,129},{129,193},{2,66},{66,130... | collective-permute-start | bytes 884744 | tf_op jit(solution)/shard_map/ppermute | solution.py:15
  3.0 10.7 %collective-permute-start.1 = (bf16[3,128,384]{2,1,0:T(8,128)(2,1)S(1)}, bf16[3,128,384]{2,1,0:T(8,128)(2,1)S(1)}, u32[]{:S(2)}, u32[]{:S(2)}) collective-permute-start(bf16[3,128,384]{2,1,0:T(8,128)(2,1)S(1)} %get-tuple-element.61), channel_id=1, source_target_pairs={{64,0},{128,64},{192,128},{65,1},{129,65},{193,129},{66,2},{130,66... | collective-permute-start | bytes 884744 | tf_op jit(solution)/shard_map/ppermute | solution.py:17
  7.7 29.7 %copy-start.4 = (f32[384]{0:T(512)S(1)}, f32[384]{0:T(512)}, u32[]{:S(2)}) copy-start(f32[384]{0:T(512)} %param.16) | copy-start | bytes 4612
  14.6 1.9 copy-start.3
  16.6 12.7 %collective-permute-start.3 = (bf16[38,3,384]{2,1,0:T(4,128)(2,1)S(1)}, bf16[38,3,384]{2,1,0:T(4,128)(2,1)S(1)}, u32[]{:S(2)}, u32[]{:S(2)}) collective-permute-start(bf16[38,3,384]{2,1,0:T(4,128)(2,1)S(1)} %get-tuple-element.57), channel_id=1, source_target_pairs={{1,0},{2,1},{3,2},{4,3},{5,4},{6,5},{7,6},{8,7},{9,8},{10,9},{11,1... | collective-permute-start | bytes 262664 | tf_op jit(solution)/shard_map/ppermute | solution.py:17
  26.4 10.9 %collective-permute-start.2 = (bf16[38,3,384]{2,1,0:T(4,128)(2,1)S(1)}, bf16[38,3,384]{2,1,0:T(4,128)(2,1)S(1)}, u32[]{:S(2)}, u32[]{:S(2)}) collective-permute-start(bf16[38,3,384]{2,1,0:T(4,128)(2,1)S(1)} %get-tuple-element.56), channel_id=1, source_target_pairs={{0,1},{1,2},{2,3},{3,4},{4,5},{5,6},{6,7},{7,8},{8,9},{9,10},{10,1... | collective-permute-start | bytes 262664 | tf_op jit(solution)/shard_map/ppermute | solution.py:15
  132.0 4.6 %copy-start.1 = (f32[32,128,384]{2,1,0:T(8,128)S(1)}, f32[32,128,384]{2,1,0:T(8,128)}, u32[]{:S(2)}) copy-start(f32[32,128,384]{2,1,0:T(8,128)} %get-tuple-element.55) | copy-start | bytes 18874372
  132.0 4.6 %copy-start.5 = (f32[384]{0:T(512)S(1)}, f32[384]{0:T(512)}, u32[]{:S(2)}) copy-start(f32[384]{0:T(512)} %param.18) | copy-start | bytes 4612
  132.0 4.6 %copy-start.6 = (f32[384]{0:T(512)S(1)}, f32[384]{0:T(512)}, u32[]{:S(2)}) copy-start(f32[384]{0:T(512)} %param.17) | copy-start | bytes 4612
  135.8 2.3 copy-start.9
  135.8 2.3 copy-start.11
  138.1 59.8 %copy-start.2 = (bf16[32,128,384]{2,1,0:T(8,128)(2,1)S(1)}, bf16[32,128,384]{2,1,0:T(8,128)(2,1)}, u32[]{:S(2)}) copy-start(bf16[32,128,384]{2,1,0:T(8,128)(2,1)} %param.14) | copy-start | bytes 9437188
  138.1 59.8 %copy-start.10 = (bf16[1536,384]{1,0:T(8,128)(2,1)S(1)}, bf16[1536,384]{1,0:T(8,128)(2,1)}, u32[]{:S(2)}) copy-start(bf16[1536,384]{1,0:T(8,128)(2,1)} %param.21) | copy-start | bytes 3538948
  138.2 59.8 %copy-start.13 = (f32[384]{0:T(512)S(1)}, f32[384]{0:T(512)}, u32[]{:S(2)}) copy-start(f32[384]{0:T(512)} %param.22) | copy-start | bytes 4612
  138.2 59.8 %copy-start.14 = (f32[384]{0:T(512)S(1)}, f32[384]{0:T(512)}, u32[]{:S(2)}) copy-start(f32[384]{0:T(512)} %param.23) | copy-start | bytes 4612
  198.0 9.3 %copy-start.7 = (f32[384]{0:T(512)S(1)}, f32[384]{0:T(512)}, u32[]{:S(2)}) copy-start(f32[384]{0:T(512)} %param.25) | copy-start | bytes 4612
  198.0 9.3 %copy-start.8 = (f32[384]{0:T(512)S(1)}, f32[384]{0:T(512)}, u32[]{:S(2)}) copy-start(f32[384]{0:T(512)} %param.24) | copy-start | bytes 4612
  218.3 13.9 %copy-start.12 = (f32[768]{0:T(1024)S(1)}, f32[768]{0:T(1024)}, u32[]{:S(2)}) copy-start(f32[768]{0:T(1024)} %param.27) | copy-start | bytes 9220
where the time goes:
time: 289 us; the launch traced here: 288 us
  other arithmetic  105 us (36%)
  matrix products  73 us (25%)
  local copies, waits for them, and re-layouts  56.8 us (20%)
  blocking collectives  29.6 us (10%)
  starting transfers between devices  14.8 us (5%)
  waiting for transfers between devices  8.03 us (3%)
    reduce_sum x1, other arithmetic, layer_norm(): center = jnp.mean(values, axis=-1, keepdims=True)  94.6 us
    dot_general x1, matrix products, per_device(): jnp.dot(normed, expand_weight, preferred_element_type=jnp.float32)  59.8 us
    all_to_all x1, blocking collectives, per_device(): lax.all_to_all(result, 'rows', split_axis=2, concat_axis=0, tiled=True)  29.6 us
    unnamed x33, local copies, waits for them, and re-layouts  13.5 us
    reshape x2, local copies, waits for them, and re-layouts, per_device(): down_normed.reshape(half_rows, 2, half_cols, 2, channels)  13.2 us
    ppermute x2, starting transfers between devices, with_halo(): lax.ppermute(head, axis, [((i + 1) % count, i) for i in range(ends)])  11.1 us
    ppermute x2, waiting for transfers between devices, with_halo(): lax.ppermute(tail, axis, [(i, (i + 1) % count) for i in range(ends)])  8.03 us
    another operation x1, local copies, waits for them, and re-layouts, per_device(): patches.reshape(half_rows * half_cols, 4 * channels)  7.98 us
  transfers between devices with their start and end apart: 4, of which 1 were waited for; matrix products, arithmetic and copies ran while one was open for 4% of the time, Pallas kernels for 0%

commit v1 on v0

v1 whole, which is shorter than its diff:
```python
import jax
import jax.numpy as jnp
from jax import lax
from jax.experimental import pallas as pl
from jax.experimental.pallas import tpu as pltpu
from jax.sharding import PartitionSpec as P

MESH = pl.DeviceIdType.MESH
F32 = jnp.float32
BF16 = jnp.bfloat16

ROWS, COLS, C, HID, C2 = 32, 128, 384, 1536, 768
LT = C // 128
PITCH = 144
LEFT = 8
STEP = 4
STEPS = ROWS // STEP
HALF = COLS // 2
M = STEP * COLS
CHUNKS = 6
HC = HID // CHUNKS


def block_kernel(
    feat, dw, db, gain, shift, w1, b1, w2, b2, scale, dgain, dshift, wd, bd,
    out,
    xin, xp, wb, cs, nb, acc, dn, sbuf, cbuf, rowh, colh, corner,
    in_sem, row_s, row_r, col_s, col_r, cor_s, cor_r, out_s, out_r, own_sem,
):
    r = lax.axis_index("rows")
    c = lax.axis_index("cols")
    nr, nc = 4, lax.axis_size("cols")
    up, down = lax.rem(r + nr - 1, nr), lax.rem(r + 1, nr)
    left, right = lax.rem(c + nc - 1, nc), lax.rem(c + 1, nc)

    load = pltpu.make_async_copy(feat, xin, in_sem)
    load.start()

    barrier = pltpu.get_barrier_semaphore()
    partners = [(lax.rem(r + j, nr), c) for j in (1, 2, 3)]
    partners += [(r, left), (r, right)]
    partners += [(up, left), (up, right), (down, left), (down, right)]
    for who in partners:
        pl.semaphore_signal(barrier, inc=1, device_id=who, device_id_type=MESH)

    for a in range(7):
        for b in range(7):
            for t in range(LT):
                wb[t, a * 7 + b] = jnp.broadcast_to(
                    dw[a, pl.ds(b, 1), pl.ds(t * 128, 128)], (8, 128)
                )

    pl.semaphore_wait(barrier, len(partners))

    def row_copy(k):
        return pltpu.make_async_remote_copy(
            src_ref=feat.at[pl.ds(0 if k == 0 else ROWS - 3, 3)],
            dst_ref=rowh.at[1 - k],
            send_sem=row_s.at[k],
            recv_sem=row_r.at[1 - k],
            device_id=(up if k == 0 else down, c),
            device_id_type=MESH,
        )

    @pl.when(r > 0)
    def _():
        row_copy(0).start()

    @pl.when(r < nr - 1)
    def _():
        row_copy(1).start()

    load.wait()

    def fill(i, carry):
        at = pl.multiple_of((i + 3) * PITCH + LEFT, 8)
        for t in range(LT):
            xp[t, pl.ds(at, COLS), :] = xin[i, :, pl.ds(t * 128, 128)].astype(F32)
        return carry

    lax.fori_loop(0, ROWS, fill, 0)

    for side in range(2):
        for j in range(3):
            at = 3 * PITCH + LEFT + (j if side == 0 else COLS - 3 + j)
            for t in range(LT):
                cbuf[side, j, :, pl.ds(t * 128, 128)] = xp[
                    t, pl.ds(at, ROWS, stride=PITCH), :
                ].astype(BF16)

    def col_copy(side):
        return pltpu.make_async_remote_copy(
            src_ref=cbuf.at[side],
            dst_ref=colh.at[1 - side],
            send_sem=col_s.at[side],
            recv_sem=col_r.at[1 - side],
            device_id=(r, left if side == 0 else right),
            device_id_type=MESH,
        )

    def corner_copy(v, side):
        return pltpu.make_async_remote_copy(
            src_ref=cbuf.at[side, :, pl.ds(16 * v, 16)],
            dst_ref=corner.at[1 - v, 1 - side],
            send_sem=cor_s.at[v, side],
            recv_sem=cor_r.at[1 - v, 1 - side],
            device_id=(up if v == 0 else down, left if side == 0 else right),
            device_id_type=MESH,
        )

    for side in range(2):
        col_copy(side).start()
    for v in range(2):
        for side in range(2):
            corner_copy(v, side).start()

    has = [(c > 0).astype(F32), (c < nc - 1).astype(F32)]
    for side in range(2):
        col_copy(1 - side).wait_recv()
        for j in range(3):
            at = 3 * PITCH + (LEFT - 3 + j if side == 0 else LEFT + COLS + j)
            for t in range(LT):
                xp[t, pl.ds(at, ROWS, stride=PITCH), :] = (
                    colh[side, j, :, pl.ds(t * 128, 128)].astype(F32) * has[side]
                )

    def fill_rows():
        for v in range(2):
            base = 0 if v == 0 else ROWS + 3
            inside = r > 0 if v == 0 else r < nr - 1
            for side in range(2):
                corner_copy(1 - v, 1 - side).wait_recv()

            @pl.when(inside)
            def _():
                row_copy(1 - v).wait_recv()
                for i in range(3):
                    for t in range(LT):
                        xp[t, pl.ds((base + i) * PITCH + LEFT, COLS), :] = rowh[
                            v, i, :, pl.ds(t * 128, 128)
                        ].astype(F32)
                for side in range(2):
                    for j in range(3):
                        at = base * PITCH + (LEFT - 3 + j if side == 0 else LEFT + COLS + j)
                        for t in range(LT):
                            piece = (
                                corner[v, side, j, :, pl.ds(t * 128, 128)].astype(F32) * has[side]
                            )
                            for i in range(3):
                                row = (13 if v == 0 else 0) + i
                                xp[t, pl.ds(at + i * PITCH, 1), :] = piece[row : row + 1]

            @pl.when(jnp.logical_not(inside))
            def _():
                for i in range(3):
                    for t in range(LT):
                        xp[t, pl.ds((base + i) * PITCH, PITCH), :] = jnp.zeros((PITCH, 128), F32)

    def conv_part(n, s):
        t = n // 2
        for q in range(4):
            jb = lax.rem(n, 2) * 4 + q
            total = [[None] * STEP, [None] * STEP]
            for o in range(8):
                x = [
                    xp[t, pl.ds((s * STEP + i) * PITCH + jb * 16 + (LEFT - 3 + o), 8, stride=2), :]
                    for i in range(STEP + 6)
                ]
                for par in range(2):
                    b = o - par
                    if 0 <= b <= 6:
                        for a in range(7):
                            w = wb[t, a * 7 + b]
                            for i in range(STEP):
                                p = x[i + a] * w
                                total[par][i] = p if total[par][i] is None else total[par][i] + p
            for par in range(2):
                for i in range(STEP):
                    at = pl.multiple_of((i * 2 + par) * HALF + jb * 8, 8)
                    cs[t, pl.ds(at, 8), :] = total[par][i]

    def mlp_part(n):
        z = jnp.dot(nb[...], w1[:, pl.ds(pl.multiple_of(n * HC, HC), HC)], preferred_element_type=F32)
        z = z + b1[:, pl.ds(pl.multiple_of(n * HC, HC), HC)]
        h = (z + z * lax.erf(z * 0.7071067811865476)).astype(BF16)
        acc[...] += jnp.dot(h, w2[pl.ds(pl.multiple_of(n * HC, HC), HC), :], preferred_element_type=F32)

    def norm(x):
        center = jnp.sum(x[0] + x[1] + x[2], axis=-1, keepdims=True) * (1.0 / C)
        x = [v - center for v in x]
        spread = jnp.sum(x[0] * x[0] + x[1] * x[1] + x[2] * x[2], axis=-1, keepdims=True) * (1.0 / C)
        f = lax.rsqrt(spread + 1e-06)
        return [v * f for v in x]

    def norm_part():
        def one(m, carry):
            at = pl.ds(pl.multiple_of(m * 64, 64), 64)
            y = norm([cs[t, at, :] + db[:, pl.ds(t * 128, 128)] for t in range(LT)])
            for t in range(LT):
                lanes = pl.ds(t * 128, 128)
                nb[at, lanes] = (y[t] * gain[:, lanes] + shift[:, lanes]).astype(BF16)
                acc[at, lanes] = jnp.zeros((64, 128), F32)
            return carry

        lax.fori_loop(0, M // 64, one, 0)

    def down_part(k, s):
        def one(m, carry):
            i, par = m // 2, lax.rem(m, 2)
            at = pl.ds(pl.multiple_of(m * 64, 64), 64)
            x = []
            for t in range(LT):
                lanes = pl.ds(t * 128, 128)
                f = xp[t, pl.ds((s * STEP + i + 3) * PITCH + LEFT + par, HALF, stride=2), :]
                v = f + scale[:, lanes] * (0.5 * acc[at, lanes] + b2[:, lanes])
                x.append(v.astype(BF16).astype(F32))
            y = norm(x)
            for t in range(LT):
                lanes = pl.ds(t * 128, 128)
                dn[m, :, lanes] = (y[t] * dgain[:, lanes] + dshift[:, lanes]).astype(BF16)
            return carry

        lax.fori_loop(0, 2 * STEP, one, 0)
        low = lax.broadcasted_iota(jnp.int32, (HALF, 128), 1) < 64
        patches = jnp.concatenate(
            [jnp.concatenate([dn[4 * p + e] for e in range(4)], axis=1) for p in range(2)], axis=0
        )
        res = jnp.dot(patches, wd[...], preferred_element_type=F32) + bd[...]
        for d in range(4):
            tile = (0, 2, 3, 5)[d] * 128
            for p in range(2):
                sbuf[d, k, p] = res[p * HALF : (p + 1) * HALF, tile : tile + 128].astype(BF16)
        for g in range(2):
            tile = (1, 4)[g] * 128
            e0, e1 = res[:HALF, tile : tile + 128], res[HALF:, tile : tile + 128]
            sbuf[2 * g, k, 2] = jnp.where(low, e0, pltpu.roll(e1, 64, 1)).astype(BF16)
            sbuf[2 * g + 1, k, 2] = jnp.where(low, pltpu.roll(e0, 64, 1), e1).astype(BF16)
        for d in range(4):
            @pl.when(r != d)
            def _():
                out_copy(d, k, s).start()

            @pl.when(r == d)
            def _():
                own_copy(d, k, s).start()

    def out_copy(d, k, s):
        return pltpu.make_async_remote_copy(
            src_ref=sbuf.at[d, k],
            dst_ref=out.at[r, s],
            send_sem=out_s.at[d, k],
            recv_sem=out_r.at[r, k],
            device_id=(d, c),
            device_id_type=MESH,
        )

    def in_copy(src, k, s):
        return pltpu.make_async_remote_copy(
            src_ref=sbuf.at[src, k],
            dst_ref=out.at[src, s],
            send_sem=out_s.at[src, k],
            recv_sem=out_r.at[src, k],
            device_id=(src, c),
            device_id_type=MESH,
        )

    def own_copy(d, k, s):
        return pltpu.make_async_copy(sbuf.at[d, k], out.at[d, s], own_sem.at[k])

    def rows_of(k):
        return lax.rem(k + 1, STEPS)

    def conv_only(n, carry):
        conv_part(n, rows_of(0))
        return carry

    lax.fori_loop(0, CHUNKS, conv_only, 0)
    norm_part()

    def step(k, carry):
        @pl.when(k == STEPS - 2)
        def _():
            fill_rows()

        s = rows_of(k)

        def both(n, carry2):
            conv_part(n, s)
            mlp_part(n)
            return carry2

        lax.fori_loop(0, CHUNKS, both, 0)
        down_part(k - 1, rows_of(k - 1))
        norm_part()
        return carry

    lax.fori_loop(1, STEPS, step, 0)

    def mlp_only(n, carry):
        mlp_part(n)
        return carry

    lax.fori_loop(0, CHUNKS, mlp_only, 0)
    down_part(STEPS - 1, rows_of(STEPS - 1))

    @pl.when(r > 0)
    def _():
        row_copy(0).wait_send()

    @pl.when(r < nr - 1)
    def _():
        row_copy(1).wait_send()

    for side in range(2):
        col_copy(side).wait_send()
        for v in range(2):
            corner_copy(v, side).wait_send()

    def finish(k, carry):
        s = rows_of(k)
        for d in range(4):
            @pl.when(r != d)
            def _():
                in_copy(d, k, s).wait_recv()
                out_copy(d, k, s).wait_send()

            @pl.when(r == d)
            def _():
                own_copy(d, k, s).wait()

        return carry

    lax.fori_loop(0, STEPS, finish, 0)


def unpack_kernel(packed, out):
    odd = lax.rem(lax.axis_index("rows"), 2)

    @pl.when(odd == 0)
    def _():
        for s in range(STEPS):
            for p in range(2):
                tail = packed[0, s, 2][:, p * 64 : (p + 1) * 64]
                out[2 * s + p] = jnp.concatenate([packed[0, s, p], tail], axis=1)

    @pl.when(odd == 1)
    def _():
        for s in range(STEPS):
            for p in range(2):
                head = packed[0, s, 2][:, p * 64 : (p + 1) * 64]
                out[2 * s + p] = jnp.concatenate([head, packed[0, s, p]], axis=1)


def per_device(
    features, depth_weight, depth_bias, norm_gain, norm_shift, expand_weight, expand_bias,
    reduce_weight, reduce_bias, layer_scale, down_gain, down_shift, down_weight, down_bias,
):
    row = lambda v: v.reshape(1, -1)
    vmem = pl.BlockSpec(memory_space=pltpu.VMEM)
    anywhere = pl.BlockSpec(memory_space=pl.ANY)
    dma = pltpu.SemaphoreType.DMA
    packed = pl.pallas_call(
        block_kernel,
        out_shape=jax.ShapeDtypeStruct((4, STEPS, 3, HALF, 128), BF16),
        in_specs=[anywhere] + [vmem] * 13,
        out_specs=anywhere,
        scratch_shapes=[
            pltpu.VMEM((ROWS, COLS, C), BF16),
            pltpu.VMEM((LT, (ROWS + 6) * PITCH, 128), F32),
            pltpu.VMEM((LT, 49, 8, 128), F32),
            pltpu.VMEM((LT, M, 128), F32),
            pltpu.VMEM((M, C), BF16),
            pltpu.VMEM((M, C), F32),
            pltpu.VMEM((2 * STEP, HALF, C), BF16),
            pltpu.VMEM((4, STEPS, 3, HALF, 128), BF16),
            pltpu.VMEM((2, 3, ROWS, C), BF16),
            pltpu.VMEM((2, 3, COLS, C), BF16),
            pltpu.VMEM((2, 3, ROWS, C), BF16),
            pltpu.VMEM((2, 2, 3, 16, C), BF16),
            dma, dma((2,)), dma((2,)), dma((2,)), dma((2,)), dma((2, 2)), dma((2, 2)),
            dma((4, STEPS)), dma((4, STEPS)), dma((STEPS,)),
        ],
        compiler_params=pltpu.CompilerParams(
            collective_id=0, has_side_effects=True, vmem_limit_bytes=56 * 2**20
        ),
    )(
        features, depth_weight, row(depth_bias), row(norm_gain), row(norm_shift), expand_weight,
        row(expand_bias), reduce_weight, row(reduce_bias), row(layer_scale), row(down_gain),
        row(down_shift), down_weight.reshape(4 * C, C2), row(down_bias),
    )
    return pl.pallas_call(
        unpack_kernel,
        grid=(4,),
        out_shape=jax.ShapeDtypeStruct((64, HALF, C2 // 4), BF16),
        in_specs=[pl.BlockSpec((1, STEPS, 3, HALF, 128), lambda i: (i, 0, 0, 0, 0))],
        out_specs=pl.BlockSpec((16, HALF, C2 // 4), lambda i: (i, 0, 0)),
    )(packed)


def solution(mesh):
    in_specs = (P("rows", "cols", None),) + (P(),) * 13
    return jax.shard_map(
        per_device, mesh=mesh, in_specs=in_specs, out_specs=P(None, "cols", "rows"), check_vma=False
    )
```

time: 289 us -> 117 us (0.40)
  the two profiles are of different devices: /device:TPU:8 before, /device:TPU:1 now
where the time goes in v1:
time: 117 us; the launch traced here: 116 us
  Pallas kernels  105 us (90%)
  local copies, waits for them, and re-layouts  11.4 us (10%)
    pallas_call x1, Pallas kernels, per_device(): pl.pallas_call(block_kernel, out_shape=jax.ShapeDtypeStruct((4, STEPS, 3,...  101 us
    reshape x9, local copies, waits for them, and re-layouts, per_device(): row = lambda v: v.reshape(1, -1)  11.4 us
    pallas_call x1, Pallas kernels, per_device(): pl.pallas_call(unpack_kernel, grid=(4,), out_shape=jax.ShapeDtypeStruct((...  3.95 us

profile of v1, /device:TPU:1, one launch (start us, length us, event | category | flops | bytes accessed | tf_op | source)
XLA Modules:
  0.0 116.4 jit_solution(1623003510425734474)
XLA Ops:
  0.0 1.3 %reshape.30.db = f32[1,384]{1,0:T(1,128)} reshape(f32[384]{0:T(512)} %param.16) | data formatting | bytes 3072 | tf_op jit(solution)/shard_map/reshape | solution.py:358
  1.3 1.2 %reshape.31.gain = f32[1,384]{1,0:T(1,128)} reshape(f32[384]{0:T(512)} %param.17) | data formatting | bytes 3072 | tf_op jit(solution)/shard_map/reshape | solution.py:358
  2.5 1.3 %reshape.32.shift = f32[1,384]{1,0:T(1,128)} reshape(f32[384]{0:T(512)} %param.18) | data formatting | bytes 3072 | tf_op jit(solution)/shard_map/reshape | solution.py:358
  3.8 1.3 %reshape.34.b2 = f32[1,384]{1,0:T(1,128)} reshape(f32[384]{0:T(512)} %param.22) | data formatting | bytes 3072 | tf_op jit(solution)/shard_map/reshape | solution.py:358
  5.0 1.3 %reshape.35.scale = f32[1,384]{1,0:T(1,128)} reshape(f32[384]{0:T(512)} %param.23) | data formatting | bytes 3072 | tf_op jit(solution)/shard_map/reshape | solution.py:358
  6.3 1.3 %reshape.36.dgain = f32[1,384]{1,0:T(1,128)} reshape(f32[384]{0:T(512)} %param.24) | data formatting | bytes 3072 | tf_op jit(solution)/shard_map/reshape | solution.py:358
  7.6 1.3 %reshape.37.dshift = f32[1,384]{1,0:T(1,128)} reshape(f32[384]{0:T(512)} %param.25) | data formatting | bytes 3072 | tf_op jit(solution)/shard_map/reshape | solution.py:358
  8.8 1.3 %reshape.39.bd = f32[1,768]{1,0:T(1,128)} reshape(f32[768]{0:T(1024)} %param.27) | data formatting | bytes 6144 | tf_op jit(solution)/shard_map/reshape | solution.py:358
  10.1 1.3 %reshape.33.b1 = f32[1,1536]{1,0:T(1,128)} reshape(f32[1536]{0:T(1024)} %param.20) | data formatting | bytes 12288 | tf_op jit(solution)/shard_map/reshape | solution.py:358
  11.4 101.0 %shard_map.136.packed = bf16[4,8,3,64,128]{4,3,2,1,0:T(8,128)(2,1)} custom-call(bf16[32,128,384]{2,1,0:T(8,128)(2,1)} %feat.1, f32[7,7,384]{2,1,0:T(8,128)} %dw.1, f32[1,384]{1,0:T(1,128)} %reshape.30.db, f32[1,384]{1,0:T(1,128)} %reshape.31.gain, f32[1,384]{1,0:T(1,128)} %reshape.32.shift, bf16[384,1536]{1,0:T(8,128)(2,1)} %w1.1, f32[1,1536]{1,0:T(1,128)} %reshape.33.b1, ...), custom_call_target="tpu_custom_call" | custom-call | tf_op jit(solution)/shard_map/pallas_call | solution.py:362
  112.4 4.0 %shard_map.137 = bf16[64,64,192]{2,1,0:T(8,128)(2,1)} custom-call(bf16[4,8,3,64,128]{4,3,2,1,0:T(8,128)(2,1)} %shard_map.136.packed), custom_call_target="tpu_custom_call" | custom-call | tf_op jit(solution)/shard_map/pallas_call | solution.py:391

commit v2 on v1

v2 whole, which is shorter than its diff:
```python
import jax
import jax.numpy as jnp
from jax import lax
from jax.experimental import pallas as pl
from jax.experimental.pallas import tpu as pltpu
from jax.sharding import PartitionSpec as P

MESH = pl.DeviceIdType.MESH
F32 = jnp.float32
BF16 = jnp.bfloat16

ROWS, COLS, C, HID, C2 = 32, 128, 384, 1536, 768
LT = C // 128
PITCH = 144
LEFT = 8
STEP = 4
STEPS = ROWS // STEP
HALF = COLS // 2
M = STEP * COLS
CHUNKS = 6
HC = HID // CHUNKS


def block_kernel(
    feat, dw_hbm, db, gain, shift, w1_hbm, b1_hbm, w2_hbm, b2, scale, dgain, dshift, wd_hbm, bd_hbm,
    out,
    xin, xp, dw, v0, v1, v2, v3, v4, v5, v6, b1_in, bd_in, wb, pv, b1, bd, w1, w2, wd, nb_new, nb, acc, acc_done, patches, sbuf,
    cbuf, rowh, colh, corner,
    in_sem, w_sem, p_sem, row_s, row_r, col_s, col_r, cor_s, cor_r, out_s, out_r, own_sem,
):
    r = lax.axis_index("rows")
    c = lax.axis_index("cols")
    nr, nc = 4, lax.axis_size("cols")
    up, down = lax.rem(r + nr - 1, nr), lax.rem(r + 1, nr)
    left, right = lax.rem(c + nc - 1, nc), lax.rem(c + 1, nc)

    barrier = pltpu.get_barrier_semaphore()
    partners = [(lax.rem(r + j, nr), c) for j in (1, 2, 3)]
    partners += [(r, left), (r, right)]
    partners += [(up, left), (up, right), (down, left), (down, right)]
    for who in partners:
        pl.semaphore_signal(barrier, inc=1, device_id=who, device_id_type=MESH)

    spans = [(0, 16), (COLS - 16, 16), (16, COLS - 32)]
    loads = [
        pltpu.make_async_copy(
            feat.at[:, pl.ds(at, size)], xin.at[:, pl.ds(at, size)], in_sem.at[n]
        )
        for n, (at, size) in enumerate(spans)
    ]
    loads += [
        pltpu.make_async_copy(src, dst, w_sem.at[n])
        for n, (src, dst) in enumerate([(w1_hbm, w1), (w2_hbm, w2), (wd_hbm, wd)])
    ]
    vecs = (v0, v1, v2, v3, v4, v5, v6)
    small = list(zip((db, gain, shift, b2, scale, dgain, dshift), vecs))
    small += [(dw_hbm, dw), (b1_hbm, b1_in), (bd_hbm, bd_in)]
    small = [pltpu.make_async_copy(src, dst, p_sem.at[n]) for n, (src, dst) in enumerate(small)]
    for load in loads[:2] + small + loads[2:]:
        load.start()

    def vec(n, t):
        return pv[pl.ds(n, 1), pl.ds(t * 128, 128)]

    def fill(span):
        at, size = span

        def one(i, carry):
            to = pl.multiple_of((i + 3) * PITCH + LEFT + at, 8)
            for t in range(LT):
                xp[t, pl.ds(to, size), :] = xin[i, pl.ds(at, size), pl.ds(t * 128, 128)].astype(F32)
            return carry

        lax.fori_loop(0, ROWS, one, 0, unroll=4)

    for side in range(2):
        loads[side].wait()
        fill(spans[side])
        for j in range(3):
            at = 3 * PITCH + LEFT + (j if side == 0 else COLS - 3 + j)
            for t in range(LT):
                cbuf[side, j, :, pl.ds(t * 128, 128)] = xp[
                    t, pl.ds(at, ROWS, stride=PITCH), :
                ].astype(BF16)

    pl.semaphore_wait(barrier, len(partners))

    def col_copy(side):
        return pltpu.make_async_remote_copy(
            src_ref=cbuf.at[side],
            dst_ref=colh.at[1 - side],
            send_sem=col_s.at[side],
            recv_sem=col_r.at[1 - side],
            device_id=(r, left if side == 0 else right),
            device_id_type=MESH,
        )

    def corner_copy(v, side):
        return pltpu.make_async_remote_copy(
            src_ref=cbuf.at[side, :, pl.ds(16 * v, 16)],
            dst_ref=corner.at[1 - v, 1 - side],
            send_sem=cor_s.at[v, side],
            recv_sem=cor_r.at[1 - v, 1 - side],
            device_id=(up if v == 0 else down, left if side == 0 else right),
            device_id_type=MESH,
        )

    def row_copy(k):
        return pltpu.make_async_remote_copy(
            src_ref=feat.at[pl.ds(0 if k == 0 else ROWS - 3, 3)],
            dst_ref=rowh.at[1 - k],
            send_sem=row_s.at[k],
            recv_sem=row_r.at[1 - k],
            device_id=(up if k == 0 else down, c),
            device_id_type=MESH,
        )

    for side in range(2):
        col_copy(side).start()
    for v in range(2):
        for side in range(2):
            corner_copy(v, side).start()

    @pl.when(r > 0)
    def _():
        row_copy(0).start()

    @pl.when(r < nr - 1)
    def _():
        row_copy(1).start()

    for load in small:
        load.wait()
    for a in range(7):
        for b in range(7):
            for t in range(LT):
                wb[t, a * 7 + b] = jnp.broadcast_to(
                    dw[a, pl.ds(b, 1), pl.ds(t * 128, 128)], (8, 128)
                )
    for n in range(7):
        pv[pl.ds(n, 1), :] = vecs[n][...].reshape(1, C)
    b1[...] = b1_in[...].reshape(1, HID)
    bd[...] = bd_in[...].reshape(1, C2)

    loads[2].wait()
    fill(spans[2])

    has = [(c > 0).astype(F32), (c < nc - 1).astype(F32)]

    def fill_cols():
        for side in range(2):
            col_copy(1 - side).wait_recv()
            for j in range(3):
                at = 3 * PITCH + (LEFT - 3 + j if side == 0 else LEFT + COLS + j)
                for t in range(LT):
                    xp[t, pl.ds(at, ROWS, stride=PITCH), :] = (
                        colh[side, j, :, pl.ds(t * 128, 128)].astype(F32) * has[side]
                    )

    def fill_rows():
        for v in range(2):
            base = 0 if v == 0 else ROWS + 3
            inside = r > 0 if v == 0 else r < nr - 1
            for side in range(2):
                corner_copy(1 - v, 1 - side).wait_recv()

            @pl.when(inside)
            def _():
                row_copy(1 - v).wait_recv()
                for i in range(3):
                    for t in range(LT):
                        xp[t, pl.ds((base + i) * PITCH + LEFT, COLS), :] = rowh[
                            v, i, :, pl.ds(t * 128, 128)
                        ].astype(F32)
                for side in range(2):
                    for j in range(3):
                        at = base * PITCH + (LEFT - 3 + j if side == 0 else LEFT + COLS + j)
                        for t in range(LT):
                            piece = (
                                corner[v, side, j, :, pl.ds(t * 128, 128)].astype(F32) * has[side]
                            )
                            for i in range(3):
                                row = (13 if v == 0 else 0) + i
                                xp[t, pl.ds(at + i * PITCH, 1), :] = piece[row : row + 1]

            @pl.when(jnp.logical_not(inside))
            def _():
                for i in range(3):
                    for t in range(LT):
                        xp[t, pl.ds((base + i) * PITCH, PITCH), :] = jnp.zeros((PITCH, 128), F32)

    def norm(x):
        center = jnp.sum(x[0] + x[1] + x[2], axis=-1, keepdims=True) * (1.0 / C)
        x = [v - center for v in x]
        spread = jnp.sum(x[0] * x[0] + x[1] * x[1] + x[2] * x[2], axis=-1, keepdims=True) * (1.0 / C)
        f = lax.rsqrt(spread + 1e-06)
        return [v * f for v in x]

    def conv_part(jb, s):
        whole = []
        for t in range(LT):
            total = [[None] * 2 for _ in range(STEP)]
            for o in range(8):
                x = [
                    xp[t, pl.ds((s * STEP + i) * PITCH + jb * 16 + (LEFT - 3 + o), 8, stride=2), :]
                    for i in range(STEP + 6)
                ]
                for par in range(2):
                    b = o - par
                    if 0 <= b <= 6:
                        for a in range(7):
                            w = wb[t, a * 7 + b]
                            for i in range(STEP):
                                p = x[i + a] * w
                                before = total[i][par]
                                total[i][par] = p if before is None else before + p
            whole.append(
                jnp.concatenate([total[i][par] for i in range(STEP) for par in range(2)], axis=0)
                + vec(0, t)
            )
        y = norm(whole)
        at = pl.ds(pl.multiple_of(jb * 64, 64), 64)
        for t in range(LT):
            nb_new[at, pl.ds(t * 128, 128)] = (y[t] * vec(1, t) + vec(2, t)).astype(BF16)

    def mlp_part(n):
        at = pl.ds(pl.multiple_of(n * HC, HC), HC)
        z = jnp.dot(nb[...], w1[:, at], preferred_element_type=F32) + b1[:, at]
        h = (z + z * lax.erf(z * 0.7071067811865476)).astype(BF16)
        acc[...] += jnp.dot(h, w2[at, :], preferred_element_type=F32)

    def turn():
        nb[...] = nb_new[...]
        acc_done[...] = acc[...]
        acc[...] = jnp.zeros_like(acc)

    def norm_part(jb, s):
        at = pl.ds(pl.multiple_of(jb * 64, 64), 64)
        x = []
        for t in range(LT):
            f = jnp.concatenate(
                [
                    xp[t, pl.ds((s * STEP + i + 3) * PITCH + jb * 16 + (LEFT + par), 8, stride=2), :]
                    for i in range(STEP)
                    for par in range(2)
                ],
                axis=0,
            )
            v = f + vec(4, t) * (0.5 * acc_done[at, pl.ds(t * 128, 128)] + vec(3, t))
            x.append(v.astype(BF16).astype(F32))
        y = norm(x)
        for t in range(LT):
            v = y[t] * vec(5, t) + vec(6, t)
            for a in range(2):
                for par in range(2):
                    e = a * 2 + par
                    both = jnp.concatenate([v[e * 8 : e * 8 + 8], v[e * 8 + 32 : e * 8 + 40]], axis=0)
                    patches[
                        pl.ds(pl.multiple_of(jb * 16, 16), 16), pl.ds(e * C + t * 128, 128)
                    ] = both.astype(BF16)

    def down_part(k, s):
        low = lax.broadcasted_iota(jnp.int32, (HALF, 128), 1) < 64
        res = jnp.dot(patches[...], wd[...], preferred_element_type=F32) + bd[...]

        def piece(p, tile):
            return jnp.concatenate(
                [res[q * 16 + p * 8 : q * 16 + p * 8 + 8, tile * 128 : tile * 128 + 128] for q in range(8)],
                axis=0,
            )

        for d in range(4):
            for p in range(2):
                sbuf[d, k, p] = piece(p, (0, 2, 3, 5)[d]).astype(BF16)
        for g in range(2):
            e0, e1 = piece(0, (1, 4)[g]), piece(1, (1, 4)[g])
            sbuf[2 * g, k, 2] = jnp.where(low, e0, pltpu.roll(e1, 64, 1)).astype(BF16)
            sbuf[2 * g + 1, k, 2] = jnp.where(low, pltpu.roll(e0, 64, 1), e1).astype(BF16)
        for d in range(4):
            @pl.when(r != d)
            def _():
                out_copy(d, k, s).start()

            @pl.when(r == d)
            def _():
                own_copy(d, k, s).start()

    def out_copy(d, k, s):
        return pltpu.make_async_remote_copy(
            src_ref=sbuf.at[d, k],
            dst_ref=out.at[r, s],
            send_sem=out_s.at[d, k],
            recv_sem=out_r.at[r, k],
            device_id=(d, c),
            device_id_type=MESH,
        )

    def in_copy(src, k, s):
        return pltpu.make_async_remote_copy(
            src_ref=sbuf.at[src, k],
            dst_ref=out.at[src, s],
            send_sem=out_s.at[src, k],
            recv_sem=out_r.at[src, k],
            device_id=(src, c),
            device_id_type=MESH,
        )

    def own_copy(d, k, s):
        return pltpu.make_async_copy(sbuf.at[d, k], out.at[d, s], own_sem.at[k])

    def rows_of(k):
        return lax.rem(k + 1, STEPS)

    def first(q, carry):
        @pl.when(q == 6)
        def _():
            fill_cols()

        conv_part(jnp.where(q == 6, 0, jnp.where(q == 7, 7, q + 1)), rows_of(0))
        return carry

    lax.fori_loop(0, 8, first, 0)
    for load in loads[3:]:
        load.wait()
    acc[...] = jnp.zeros_like(acc)
    acc_done[...] = jnp.zeros_like(acc)
    nb[...] = nb_new[...]

    def step(k, carry):
        @pl.when(k == STEPS - 2)
        def _():
            fill_rows()

        s = rows_of(k)
        s_old = rows_of(k + STEPS - 2)

        def part(h, carry2):
            for q in range(4):
                conv_part(h * 4 + q, s)
                if q < 3:
                    mlp_part(h * 3 + q)
                norm_part(h * 4 + q, s_old)
            return carry2

        lax.fori_loop(0, 2, part, 0)

        @pl.when(k >= 2)
        def _():
            down_part(k - 2, s_old)

        turn()
        return carry

    lax.fori_loop(1, STEPS, step, 0)

    def late(h, carry):
        for q in range(4):
            if q < 3:
                mlp_part(h * 3 + q)
            norm_part(h * 4 + q, rows_of(STEPS - 2))
        return carry

    lax.fori_loop(0, 2, late, 0)
    down_part(STEPS - 2, rows_of(STEPS - 2))
    turn()

    def last(h, carry):
        for q in range(4):
            norm_part(h * 4 + q, rows_of(STEPS - 1))
        return carry

    lax.fori_loop(0, 2, last, 0)
    down_part(STEPS - 1, rows_of(STEPS - 1))

    @pl.when(r > 0)
    def _():
        row_copy(0).wait_send()

    @pl.when(r < nr - 1)
    def _():
        row_copy(1).wait_send()

    for side in range(2):
        col_copy(side).wait_send()
        for v in range(2):
            corner_copy(v, side).wait_send()

    def finish(k, carry):
        s = rows_of(k)
        for d in range(4):
            @pl.when(r != d)
            def _():
                in_copy(d, k, s).wait_recv()
                out_copy(d, k, s).wait_send()

            @pl.when(r == d)
            def _():
                own_copy(d, k, s).wait()

        return carry

    lax.fori_loop(0, STEPS, finish, 0)


def unpack_kernel(packed, out):
    odd = lax.rem(lax.axis_index("rows"), 2)

    @pl.when(odd == 0)
    def _():
        for s in range(STEPS):
            for p in range(2):
                tail = packed[0, s, 2][:, p * 64 : (p + 1) * 64]
                out[2 * s + p] = jnp.concatenate([packed[0, s, p], tail], axis=1)

    @pl.when(odd == 1)
    def _():
        for s in range(STEPS):
            for p in range(2):
                head = packed[0, s, 2][:, p * 64 : (p + 1) * 64]
                out[2 * s + p] = jnp.concatenate([head, packed[0, s, p]], axis=1)


def per_device(
    features, depth_weight, depth_bias, norm_gain, norm_shift, expand_weight, expand_bias,
    reduce_weight, reduce_bias, layer_scale, down_gain, down_shift, down_weight, down_bias,
):
    anywhere = pl.BlockSpec(memory_space=pl.ANY)
    dma = pltpu.SemaphoreType.DMA
    packed = pl.pallas_call(
        block_kernel,
        out_shape=jax.ShapeDtypeStruct((4, STEPS, 3, HALF, 128), BF16),
        in_specs=[anywhere] * 14,
        out_specs=anywhere,
        scratch_shapes=[
            pltpu.VMEM((ROWS, COLS, C), BF16),
            pltpu.VMEM((LT, (ROWS + 6) * PITCH, 128), F32),
            pltpu.VMEM((7, 7, C), F32),
            *[pltpu.VMEM((C,), F32) for _ in range(7)],
            pltpu.VMEM((HID,), F32),
            pltpu.VMEM((C2,), F32),
            pltpu.VMEM((LT, 49, 8, 128), F32),
            pltpu.VMEM((8, C), F32),
            pltpu.VMEM((1, HID), F32),
            pltpu.VMEM((1, C2), F32),
            pltpu.VMEM((C, HID), BF16),
            pltpu.VMEM((HID, C), BF16),
            pltpu.VMEM((4 * C, C2), BF16),
            pltpu.VMEM((M, C), BF16),
            pltpu.VMEM((M, C), BF16),
            pltpu.VMEM((M, C), F32),
            pltpu.VMEM((M, C), F32),
            pltpu.VMEM((2 * HALF, 4 * C), BF16),
            pltpu.VMEM((4, STEPS, 3, HALF, 128), BF16),
            pltpu.VMEM((2, 3, ROWS, C), BF16),
            pltpu.VMEM((2, 3, COLS, C), BF16),
            pltpu.VMEM((2, 3, ROWS, C), BF16),
            pltpu.VMEM((2, 2, 3, 16, C), BF16),
            dma((3,)), dma((3,)), dma((10,)), dma((2,)), dma((2,)), dma((2,)), dma((2,)), dma((2, 2)), dma((2, 2)),
            dma((4, STEPS)), dma((4, STEPS)), dma((STEPS,)),
        ],
        compiler_params=pltpu.CompilerParams(
            collective_id=0, has_side_effects=True, vmem_limit_bytes=56 * 2**20
        ),
    )(
        features, depth_weight, depth_bias, norm_gain, norm_shift, expand_weight, expand_bias,
        reduce_weight, reduce_bias, layer_scale, down_gain, down_shift,
        down_weight.reshape(4 * C, C2), down_bias,
    )
    return pl.pallas_call(
        unpack_kernel,
        grid=(4,),
        out_shape=jax.ShapeDtypeStruct((64, HALF, C2 // 4), BF16),
        in_specs=[pl.BlockSpec((1, STEPS, 3, HALF, 128), lambda i: (i, 0, 0, 0, 0))],
        out_specs=pl.BlockSpec((16, HALF, C2 // 4), lambda i: (i, 0, 0)),
    )(packed)


def solution(mesh):
    in_specs = (P("rows", "cols", None),) + (P(),) * 13
    return jax.shard_map(
        per_device, mesh=mesh, in_specs=in_specs, out_specs=P(None, "cols", "rows"), check_vma=False
    )
```

time: 117 us -> 77.1 us (0.66)
  Pallas kernels: 105 us -> 77 us
  local copies, waits for them, and re-layouts: 11.4 us -> 0 us
    pallas_call x1, Pallas kernels: 101 us -> 73 us  [per_device(): pl.pallas_call(block_kernel, out_shape=jax.ShapeDtypeStruct((4, STEPS, 3,...]
    reshape x9 -> x0, local copies, waits for them, and re-layouts: 11.4 us -> none  [per_device(): row = lambda v: v.reshape(1, -1)]
where the time goes in v2:
time: 77.1 us; the launch traced here: 77 us
  Pallas kernels  77 us (100%)
    pallas_call x1, Pallas kernels, per_device(): pl.pallas_call(block_kernel, out_shape=jax.ShapeDtypeStruct((4, STEPS, 3,...  73 us
    pallas_call x1, Pallas kernels, per_device(): pl.pallas_call(unpack_kernel, grid=(4,), out_shape=jax.ShapeDtypeStruct((...  3.95 us

profile of v2, /device:TPU:1, one launch (start us, length us, event | category | flops | bytes accessed | tf_op | source)
XLA Modules:
  0.0 77.0 jit_solution(10736321041983006209)
XLA Ops:
  0.0 73.0 %shard_map.136.packed = bf16[4,8,3,64,128]{4,3,2,1,0:T(8,128)(2,1)} custom-call(bf16[32,128,384]{2,1,0:T(8,128)(2,1)} %feat.1, f32[7,7,384]{2,1,0:T(8,128)} %dw_hbm.1, f32[384]{0:T(512)} %db.1, f32[384]{0:T(512)} %gain.1, f32[384]{0:T(512)} %shift.1, bf16[384,1536]{1,0:T(8,128)(2,1)} %w1_hbm.1, f32[1536]{0:T(1024)} %b1_hbm.1, bf16[1536,384]{1,0:T(8,128)(2,1)} %w2_hbm.1, ...), custom_call_target="tpu_custom_call" | custom-call | tf_op jit(solution)/shard_map/pallas_call | solution.py:429
  73.0 4.0 %shard_map.137 = bf16[64,64,192]{2,1,0:T(8,128)(2,1)} custom-call(bf16[4,8,3,64,128]{4,3,2,1,0:T(8,128)(2,1)} %shard_map.136.packed), custom_call_target="tpu_custom_call" | custom-call | tf_op jit(solution)/shard_map/pallas_call | solution.py:469

commit v3 on v2

--- a/solution.py
+++ b/solution.py
@@ -24,7 +24,7 @@
 def block_kernel(
     feat, dw_hbm, db, gain, shift, w1_hbm, b1_hbm, w2_hbm, b2, scale, dgain, dshift, wd_hbm, bd_hbm,
     out,
-    xin, xp, dw, v0, v1, v2, v3, v4, v5, v6, b1_in, bd_in, wb, pv, b1, bd, w1, w2, wd, nb_new, nb, acc, acc_done, patches, sbuf,
+    xin, xp, cs, dw, v0, v1, v2, v3, v4, v5, v6, b1_in, bd_in, wb, pv, b1, bd, w1, w2, wd, nb_next, nb_new, nb, acc, acc_done, patches, sbuf,
     cbuf, rowh, colh, corner,
     in_sem, w_sem, p_sem, row_s, row_r, col_s, col_r, cor_s, cor_r, out_s, out_r, own_sem,
 ):
@@ -33,13 +33,6 @@
     nr, nc = 4, lax.axis_size("cols")
     up, down = lax.rem(r + nr - 1, nr), lax.rem(r + 1, nr)
     left, right = lax.rem(c + nc - 1, nc), lax.rem(c + 1, nc)
-
-    barrier = pltpu.get_barrier_semaphore()
-    partners = [(lax.rem(r + j, nr), c) for j in (1, 2, 3)]
-    partners += [(r, left), (r, right)]
-    partners += [(up, left), (up, right), (down, left), (down, right)]
-    for who in partners:
-        pl.semaphore_signal(barrier, inc=1, device_id=who, device_id_type=MESH)
 
     spans = [(0, 16), (COLS - 16, 16), (16, COLS - 32)]
     loads = [
@@ -59,6 +52,12 @@
     for load in loads[:2] + small + loads[2:]:
         load.start()
 
+    barrier = pltpu.get_barrier_semaphore()
+    partners = [(lax.rem(r + j, nr), c) for j in (1, 2, 3)]
+    partners += [(r, left), (r, right)]
+    for who in partners:
+        pl.semaphore_signal(barrier, inc=1, device_id=who, device_id_type=MESH)
+
     def vec(n, t):
         return pv[pl.ds(n, 1), pl.ds(t * 128, 128)]
 
@@ -83,8 +82,6 @@
                     t, pl.ds(at, ROWS, stride=PITCH), :
                 ].astype(BF16)
 
-    pl.semaphore_wait(barrier, len(partners))
-
     def col_copy(side):
         return pltpu.make_async_remote_copy(
             src_ref=cbuf.at[side],
@@ -97,11 +94,11 @@
 
     def corner_copy(v, side):
         return pltpu.make_async_remote_copy(
-            src_ref=cbuf.at[side, :, pl.ds(16 * v, 16)],
-            dst_ref=corner.at[1 - v, 1 - side],
+            src_ref=colh.at[side, :, pl.ds(16 * v, 16)],
+            dst_ref=corner.at[1 - v, side],
             send_sem=cor_s.at[v, side],
-            recv_sem=cor_r.at[1 - v, 1 - side],
-            device_id=(up if v == 0 else down, left if side == 0 else right),
+            recv_sem=cor_r.at[1 - v, side],
+            device_id=(up if v == 0 else down, c),
             device_id_type=MESH,
         )
 
@@ -115,19 +112,18 @@
             device_id_type=MESH,
         )
 
-    for side in range(2):
-        col_copy(side).start()
-    for v in range(2):
+    def send_halo():
+        pl.semaphore_wait(barrier, len(partners))
         for side in range(2):
-            corner_copy(v, side).start()
-
-    @pl.when(r > 0)
-    def _():
-        row_copy(0).start()
-
-    @pl.when(r < nr - 1)
-    def _():
-        row_copy(1).start()
+            col_copy(side).start()
+
+        @pl.when(r > 0)
+        def _():
+            row_copy(0).start()
+
+        @pl.when(r < nr - 1)
+        def _():
+            row_copy(1).start()
 
     for load in small:
         load.wait()
@@ -150,6 +146,8 @@
     def fill_cols():
         for side in range(2):
             col_copy(1 - side).wait_recv()
+            for v in range(2):
+                corner_copy(v, side).start()
             for j in range(3):
                 at = 3 * PITCH + (LEFT - 3 + j if side == 0 else LEFT + COLS + j)
                 for t in range(LT):
@@ -162,7 +160,7 @@
             base = 0 if v == 0 else ROWS + 3
             inside = r > 0 if v == 0 else r < nr - 1
             for side in range(2):
-                corner_copy(1 - v, 1 - side).wait_recv()
+                corner_copy(1 - v, side).wait_recv()
 
             @pl.when(inside)
             def _():
@@ -196,32 +194,32 @@
         f = lax.rsqrt(spread + 1e-06)
         return [v * f for v in x]
 
-    def conv_part(jb, s):
-        whole = []
+    def conv_block(jb, s, slot, t):
+        base = s * STEP * PITCH + jb * 16 + (LEFT - 3)
+        total = [[None] * 2 for _ in range(STEP)]
+        for a in range(7):
+            for i in range(STEP):
+                x = [xp[t, pl.ds(base + (i + a) * PITCH + o, 8, stride=2), :] for o in range(8)]
+                for b in range(7):
+                    w = wb[t, a * 7 + b]
+                    for par in range(2):
+                        p = x[b + par] * w
+                        before = total[i][par]
+                        total[i][par] = p if before is None else before + p
+        for i in range(STEP):
+            for par in range(2):
+                at = (i * 2 + par) * 8
+                cs[slot, t, at : at + 8, :] = total[i][par]
+
+    def conv_part(jb, s, slot):
         for t in range(LT):
-            total = [[None] * 2 for _ in range(STEP)]
-            for o in range(8):
-                x = [
-                    xp[t, pl.ds((s * STEP + i) * PITCH + jb * 16 + (LEFT - 3 + o), 8, stride=2), :]
-                    for i in range(STEP + 6)
-                ]
-                for par in range(2):
-                    b = o - par
-                    if 0 <= b <= 6:
-                        for a in range(7):
-                            w = wb[t, a * 7 + b]
-                            for i in range(STEP):
-                                p = x[i + a] * w
-                                before = total[i][par]
-                                total[i][par] = p if before is None else before + p
-            whole.append(
-                jnp.concatenate([total[i][par] for i in range(STEP) for par in range(2)], axis=0)
-                + vec(0, t)
-            )
-        y = norm(whole)
+            conv_block(jb, s, slot, t)
+
+    def norm1_part(jb, slot, to):
+        y = norm([cs[slot, t] + vec(0, t) for t in range(LT)])
         at = pl.ds(pl.multiple_of(jb * 64, 64), 64)
         for t in range(LT):
-            nb_new[at, pl.ds(t * 128, 128)] = (y[t] * vec(1, t) + vec(2, t)).astype(BF16)
+            to[at, pl.ds(t * 128, 128)] = (y[t] * vec(1, t) + vec(2, t)).astype(BF16)
 
     def mlp_part(n):
         at = pl.ds(pl.multiple_of(n * HC, HC), HC)
@@ -231,6 +229,7 @@
 
     def turn():
         nb[...] = nb_new[...]
+        nb_new[...] = nb_next[...]
         acc_done[...] = acc[...]
         acc[...] = jnp.zeros_like(acc)
 
@@ -311,58 +310,82 @@
     def rows_of(k):
         return lax.rem(k + 1, STEPS)
 
-    def first(q, carry):
-        @pl.when(q == 6)
-        def _():
-            fill_cols()
-
-        conv_part(jnp.where(q == 6, 0, jnp.where(q == 7, 7, q + 1)), rows_of(0))
-        return carry
-
-    lax.fori_loop(0, 8, first, 0)
+    def inner(k):
+        def one(n, carry):
+            jb = n // 3 + 1
+            conv_block(jb, rows_of(k), 8 * k + jb, lax.rem(n, 3))
+            return carry
+
+        lax.fori_loop(0, 18, one, 0)
+
+    def outer(k):
+        def one(n, carry):
+            jb = 7 * (n // 3)
+            conv_block(jb, rows_of(k), 8 * k + jb, lax.rem(n, 3))
+            return carry
+
+        lax.fori_loop(0, 6, one, 0)
+
+    inner(0)
+    send_halo()
+    inner(1)
+    for jb in range(1, 7):
+        norm1_part(jb, jb, nb)
+        norm1_part(jb, 8 + jb, nb_new)
+    fill_cols()
+    outer(0)
+    outer(1)
+    for jb in (0, 7):
+        norm1_part(jb, jb, nb)
+        norm1_part(jb, 8 + jb, nb_new)
     for load in loads[3:]:
         load.wait()
     acc[...] = jnp.zeros_like(acc)
     acc_done[...] = jnp.zeros_like(acc)
-    nb[...] = nb_new[...]
-
     def step(k, carry):
-        @pl.when(k == STEPS - 2)
+        @pl.when(k == STEPS - 3)
         def _():
             fill_rows()
 
-        s = rows_of(k)
+        s = rows_of(k + 1)
         s_old = rows_of(k + STEPS - 2)
 
         def part(h, carry2):
             for q in range(4):
-                conv_part(h * 4 + q, s)
+                conv_part(h * 4 + q, s, q)
+                if q < 3:
+                    mlp_part(h * 3 + q)
+                norm1_part(h * 4 + q, q, nb_next)
+                norm_part(h * 4 + q, s_old)
+            return carry2
+
+        lax.fori_loop(0, 2, part, 0)
+
+        @pl.when(k >= 2)
+        def _():
+            down_part(k - 2, s_old)
+
+        turn()
+        return carry
+
+    lax.fori_loop(1, STEPS - 1, step, 0)
+
+    def late(k, carry):
+        s_old = rows_of(k - 2)
+
+        def part(h, carry2):
+            for q in range(4):
                 if q < 3:
                     mlp_part(h * 3 + q)
                 norm_part(h * 4 + q, s_old)
             return carry2
 
         lax.fori_loop(0, 2, part, 0)
-
-        @pl.when(k >= 2)
-        def _():
-            down_part(k - 2, s_old)
-
+        down_part(k - 2, s_old)
         turn()
         return carry
 
-    lax.fori_loop(1, STEPS, step, 0)
-
-    def late(h, carry):
-        for q in range(4):
-            if q < 3:
-                mlp_part(h * 3 + q)
-            norm_part(h * 4 + q, rows_of(STEPS - 2))
-        return carry
-
-    lax.fori_loop(0, 2, late, 0)
-    down_part(STEPS - 2, rows_of(STEPS - 2))
-    turn()
+    lax.fori_loop(STEPS - 1, STEPS + 1, late, 0)
 
     def last(h, carry):
         for q in range(4):
@@ -404,20 +427,19 @@
 
 def unpack_kernel(packed, out):
     odd = lax.rem(lax.axis_index("rows"), 2)
+    parts = [(n, s, p) for n in range(2) for s in range(STEPS) for p in range(2)]
 
     @pl.when(odd == 0)
     def _():
-        for s in range(STEPS):
-            for p in range(2):
-                tail = packed[0, s, 2][:, p * 64 : (p + 1) * 64]
-                out[2 * s + p] = jnp.concatenate([packed[0, s, p], tail], axis=1)
+        for n, s, p in parts:
+            tail = packed[n, s, 2][:, p * 64 : (p + 1) * 64]
+            out[16 * n + 2 * s + p] = jnp.concatenate([packed[n, s, p], tail], axis=1)
 
     @pl.when(odd == 1)
     def _():
-        for s in range(STEPS):
-            for p in range(2):
-                head = packed[0, s, 2][:, p * 64 : (p + 1) * 64]
-                out[2 * s + p] = jnp.concatenate([head, packed[0, s, p]], axis=1)
+        for n, s, p in parts:
+            head = packed[n, s, 2][:, p * 64 : (p + 1) * 64]
+            out[16 * n + 2 * s + p] = jnp.concatenate([head, packed[n, s, p]], axis=1)
 
 
 def per_device(
@@ -434,6 +456,7 @@
         scratch_shapes=[
             pltpu.VMEM((ROWS, COLS, C), BF16),
             pltpu.VMEM((LT, (ROWS + 6) * PITCH, 128), F32),
+            pltpu.VMEM((16, LT, 64, 128), F32),
             pltpu.VMEM((7, 7, C), F32),
             *[pltpu.VMEM((C,), F32) for _ in range(7)],
             pltpu.VMEM((HID,), F32),
@@ -445,6 +468,7 @@
             pltpu.VMEM((C, HID), BF16),
             pltpu.VMEM((HID, C), BF16),
             pltpu.VMEM((4 * C, C2), BF16),
+            pltpu.VMEM((M, C), BF16),
             pltpu.VMEM((M, C), BF16),
             pltpu.VMEM((M, C), BF16),
             pltpu.VMEM((M, C), F32),
@@ -468,10 +492,10 @@
     )
     return pl.pallas_call(
         unpack_kernel,
-        grid=(4,),
+        grid=(2,),
         out_shape=jax.ShapeDtypeStruct((64, HALF, C2 // 4), BF16),
-        in_specs=[pl.BlockSpec((1, STEPS, 3, HALF, 128), lambda i: (i, 0, 0, 0, 0))],
-        out_specs=pl.BlockSpec((16, HALF, C2 // 4), lambda i: (i, 0, 0)),
+        in_specs=[pl.BlockSpec((2, STEPS, 3, HALF, 128), lambda i: (i, 0, 0, 0, 0))],
+        out_specs=pl.BlockSpec((32, HALF, C2 // 4), lambda i: (i, 0, 0)),
     )(packed)
 
 

time: 77.1 us -> 72.3 us (0.938)
  Pallas kernels: 77 us -> 72.2 us
    pallas_call x1, Pallas kernels: 73 us -> 69.4 us  [per_device(): pl.pallas_call(block_kernel, out_shape=jax.ShapeDtypeStruct((4, STEPS, 3,...]
    pallas_call x1, Pallas kernels: 3.95 us -> 2.73 us  [per_device(): pl.pallas_call(unpack_kernel, grid=(2,), out_shape=jax.ShapeDtypeStruct((...]
where the time goes in v3:
time: 72.3 us; the launch traced here: 72.2 us
  Pallas kernels  72.2 us (100%)
    pallas_call x1, Pallas kernels, per_device(): pl.pallas_call(block_kernel, out_shape=jax.ShapeDtypeStruct((4, STEPS, 3,...  69.4 us
    pallas_call x1, Pallas kernels, per_device(): pl.pallas_call(unpack_kernel, grid=(2,), out_shape=jax.ShapeDtypeStruct((...  2.73 us

profile of v3, /device:TPU:1, one launch (start us, length us, event | category | flops | bytes accessed | tf_op | source)
XLA Modules:
  0.0 72.2 jit_solution(18214975922227240587)
XLA Ops:
  0.0 69.4 %shard_map.136.packed = bf16[4,8,3,64,128]{4,3,2,1,0:T(8,128)(2,1)} custom-call(bf16[32,128,384]{2,1,0:T(8,128)(2,1)} %feat.1, f32[7,7,384]{2,1,0:T(8,128)} %dw_hbm.1, f32[384]{0:T(512)} %db.1, f32[384]{0:T(512)} %gain.1, f32[384]{0:T(512)} %shift.1, bf16[384,1536]{1,0:T(8,128)(2,1)} %w1_hbm.1, f32[1536]{0:T(1024)} %b1_hbm.1, bf16[1536,384]{1,0:T(8,128)(2,1)} %w2_hbm.1, ...), custom_call_target="tpu_custom_call" | custom-call | tf_op jit(solution)/shard_map/pallas_call | solution.py:451
  69.4 2.7 %shard_map.137 = bf16[64,64,192]{2,1,0:T(8,128)(2,1)} custom-call(bf16[4,8,3,64,128]{4,3,2,1,0:T(8,128)(2,1)} %shard_map.136.packed), custom_call_target="tpu_custom_call" | custom-call | tf_op jit(solution)/shard_map/pallas_call | solution.py:493

commit v4 on v3

--- a/solution.py
+++ b/solution.py
@@ -24,7 +24,7 @@
 def block_kernel(
     feat, dw_hbm, db, gain, shift, w1_hbm, b1_hbm, w2_hbm, b2, scale, dgain, dshift, wd_hbm, bd_hbm,
     out,
-    xin, xp, cs, dw, v0, v1, v2, v3, v4, v5, v6, b1_in, bd_in, wb, pv, b1, bd, w1, w2, wd, nb_next, nb_new, nb, acc, acc_done, patches, sbuf,
+    xin, xp, cs, dw, v0, v1, v2, v3, v4, v5, v6, b1_in, bd_in, wb, pv, b1, bd, w1, w2, wd, nb_next, nb_far, nb_new, nb, acc, acc_done, patches, sbuf,
     cbuf, rowh, colh, corner,
     in_sem, w_sem, p_sem, row_s, row_r, col_s, col_r, cor_s, cor_r, out_s, out_r, own_sem,
 ):
@@ -49,7 +49,7 @@
     small = list(zip((db, gain, shift, b2, scale, dgain, dshift), vecs))
     small += [(dw_hbm, dw), (b1_hbm, b1_in), (bd_hbm, bd_in)]
     small = [pltpu.make_async_copy(src, dst, p_sem.at[n]) for n, (src, dst) in enumerate(small)]
-    for load in loads[:2] + small + loads[2:]:
+    for load in loads[:2] + small + loads[2:3]:
         load.start()
 
     barrier = pltpu.get_barrier_semaphore()
@@ -139,6 +139,8 @@
     bd[...] = bd_in[...].reshape(1, C2)
 
     loads[2].wait()
+    for load in loads[3:]:
+        load.start()
     fill(spans[2])
 
     has = [(c > 0).astype(F32), (c < nc - 1).astype(F32)]
@@ -229,7 +231,8 @@
 
     def turn():
         nb[...] = nb_new[...]
-        nb_new[...] = nb_next[...]
+        nb_new[...] = nb_far[...]
+        nb_far[...] = nb_next[...]
         acc_done[...] = acc[...]
         acc[...] = jnp.zeros_like(acc)
 
@@ -329,34 +332,37 @@
     inner(0)
     send_halo()
     inner(1)
+    inner(2)
     for jb in range(1, 7):
-        norm1_part(jb, jb, nb)
-        norm1_part(jb, 8 + jb, nb_new)
+        for k, to in enumerate((nb, nb_new, nb_far)):
+            norm1_part(jb, 8 * k + jb, to)
     fill_cols()
-    outer(0)
-    outer(1)
+    for k in range(3):
+        outer(k)
     for jb in (0, 7):
-        norm1_part(jb, jb, nb)
-        norm1_part(jb, 8 + jb, nb_new)
+        for k, to in enumerate((nb, nb_new, nb_far)):
+            norm1_part(jb, 8 * k + jb, to)
     for load in loads[3:]:
         load.wait()
     acc[...] = jnp.zeros_like(acc)
     acc_done[...] = jnp.zeros_like(acc)
     def step(k, carry):
-        @pl.when(k == STEPS - 3)
+        @pl.when(k == STEPS - 4)
         def _():
             fill_rows()
 
-        s = rows_of(k + 1)
+        s = rows_of(k + 2)
         s_old = rows_of(k + STEPS - 2)
 
         def part(h, carry2):
+            for t in range(LT):
+                for q in range(4):
+                    conv_block(h * 4 + q, s, q, t)
+                mlp_part(h * 3 + t)
+                norm_part(h * 4 + t, s_old)
+            norm_part(h * 4 + 3, s_old)
             for q in range(4):
-                conv_part(h * 4 + q, s, q)
-                if q < 3:
-                    mlp_part(h * 3 + q)
                 norm1_part(h * 4 + q, q, nb_next)
-                norm_part(h * 4 + q, s_old)
             return carry2
 
         lax.fori_loop(0, 2, part, 0)
@@ -368,7 +374,7 @@
         turn()
         return carry
 
-    lax.fori_loop(1, STEPS - 1, step, 0)
+    lax.fori_loop(1, STEPS - 2, step, 0)
 
     def late(k, carry):
         s_old = rows_of(k - 2)
@@ -385,7 +391,7 @@
         turn()
         return carry
 
-    lax.fori_loop(STEPS - 1, STEPS + 1, late, 0)
+    lax.fori_loop(STEPS - 2, STEPS + 1, late, 0)
 
     def last(h, carry):
         for q in range(4):
@@ -456,7 +462,7 @@
         scratch_shapes=[
             pltpu.VMEM((ROWS, COLS, C), BF16),
             pltpu.VMEM((LT, (ROWS + 6) * PITCH, 128), F32),
-            pltpu.VMEM((16, LT, 64, 128), F32),
+            pltpu.VMEM((24, LT, 64, 128), F32),
             pltpu.VMEM((7, 7, C), F32),
             *[pltpu.VMEM((C,), F32) for _ in range(7)],
             pltpu.VMEM((HID,), F32),
@@ -468,6 +474,7 @@
             pltpu.VMEM((C, HID), BF16),
             pltpu.VMEM((HID, C), BF16),
             pltpu.VMEM((4 * C, C2), BF16),
+            pltpu.VMEM((M, C), BF16),
             pltpu.VMEM((M, C), BF16),
             pltpu.VMEM((M, C), BF16),
             pltpu.VMEM((M, C), BF16),

time: 72.3 us -> 70.6 us (0.976)
  Pallas kernels: 72.2 us -> 70.5 us
    pallas_call x1, Pallas kernels: 69.4 us -> 67.8 us  [per_device(): pl.pallas_call(block_kernel, out_shape=jax.ShapeDtypeStruct((4, STEPS, 3,...]
where the time goes in v4:
time: 70.6 us; the launch traced here: 70.5 us
  Pallas kernels  70.5 us (100%)
    pallas_call x1, Pallas kernels, per_device(): pl.pallas_call(block_kernel, out_shape=jax.ShapeDtypeStruct((4, STEPS, 3,...  67.8 us
    pallas_call x1, Pallas kernels, per_device(): pl.pallas_call(unpack_kernel, grid=(2,), out_shape=jax.ShapeDtypeStruct((...  2.73 us

profile of v4, /device:TPU:1, one launch (start us, length us, event | category | flops | bytes accessed | tf_op | source)
XLA Modules:
  0.0 70.5 jit_solution(10456984051039066967)
XLA Ops:
  0.0 67.8 %shard_map.136.packed = bf16[4,8,3,64,128]{4,3,2,1,0:T(8,128)(2,1)} custom-call(bf16[32,128,384]{2,1,0:T(8,128)(2,1)} %feat.1, f32[7,7,384]{2,1,0:T(8,128)} %dw_hbm.1, f32[384]{0:T(512)} %db.1, f32[384]{0:T(512)} %gain.1, f32[384]{0:T(512)} %shift.1, bf16[384,1536]{1,0:T(8,128)(2,1)} %w1_hbm.1, f32[1536]{0:T(1024)} %b1_hbm.1, bf16[1536,384]{1,0:T(8,128)(2,1)} %w2_hbm.1, ...), custom_call_target="tpu_custom_call" | custom-call | tf_op jit(solution)/shard_map/pallas_call | solution.py:457
  67.8 2.7 %shard_map.137 = bf16[64,64,192]{2,1,0:T(8,128)(2,1)} custom-call(bf16[4,8,3,64,128]{4,3,2,1,0:T(8,128)(2,1)} %shard_map.136.packed), custom_call_target="tpu_custom_call" | custom-call | tf_op jit(solution)/shard_map/pallas_call | solution.py:500
